TPU v7x, 512 devices: a whole 4x8x8 slice. The times are simulated.
512 devices in a mesh: leaf: 128 (over z, y, core), sub: 4 (over x).
Axes of the slice: x: 4, y: 8, z: 8, core: 2. Of those that a mesh axis runs over, the one named last changes fastest.
Arguments:
- light: bfloat16 [32, 1048576], P(None, ('leaf', 'sub')), may hold values from -6 to 6
- probes: bfloat16 [4, 1048576], P(None, ('leaf', 'sub')), may hold values from 0 to 1, as said below
- near_list: int32 [4096, 4], P(('leaf', 'sub')), may hold values from 0 to 4095, as said below
- far_list: int32 [4096, 32], P(('leaf', 'sub')), may hold values from 0 to 4095, as said below
- leaf_basis: bfloat16 [4096, 256, 64], P(('leaf', 'sub')), may hold values from -0.375 to 0.375
- leaf_transfer: bfloat16 [4096, 64, 64], P(('leaf', 'sub')), may hold values from -0.25 to 0.25
- far_coupling: bfloat16 [4096, 32, 64, 64], P(('leaf', 'sub')), may hold values from -0.125 to 0.125
- up_transfer: bfloat16 [3, 2, 64, 64], replicated, may hold values from -0.5 to 0.5
- upper_coupling: bfloat16 [4, 2, 64, 64], replicated, may hold values from -0.5 to 0.5
Outputs:
- irradiance: bfloat16 [32, 1048576], P(None, ('leaf', 'sub'))
Inputs may be any that keep to these rules, and one draw needn't show every extreme that they name: `near_list`: each leaf's list names 4 distinct leaves other than itself, each within 4 leaf numbers of it. `far_list`: every entry names a leaf on a device with the same sub index as the leaf's own device and another leaf index. The entries of one device's leaves name leaves of any one other device at most 4 times, and exactly 4 times for some device. `probes`: rows 0 to 2 lie in the unit box, row 3 is positive.
All inputs are finite; a program needn't handle non-finite values.
Results may differ from a plain program's by a relative error of at most 0.0049.
The roundings to bfloat16 on the way count: a program that leaves them out, or rounds other values in their place, can miss the bound.
Values may be sent and summed in bfloat16 or wider, within the bound.
A program may use at most 128 MiB of HBM per device.

v0:
```python
import jax
import jax.numpy as jnp
from jax import lax
from jax.sharding import PartitionSpec as P

HALO = 4
UPLV = 3
soften = 0.0025
spacing = 0.25


def extended(value, sides, width):
    for axis, dim in sides:
        size, length = (lax.axis_size(axis), value.shape[dim])
        up = [(i, (i + 1) % size) for i in range(size - 1)]
        down = [(j, i) for i, j in up]
        last = lax.slice_in_dim(value, length - width, length, axis=dim)
        leading = lax.slice_in_dim(value, 0, width, axis=dim)
        before = lax.ppermute(last, axis, up)
        after = lax.ppermute(leading, axis, down)
        value = jnp.concatenate([before, value, after], axis=dim)
    return value


def from_partner(value, axis, distance):
    mask = 2**distance
    pairs = [(source, source ^ mask) for source in range(lax.axis_size(axis))]
    return lax.ppermute(value, axis, pairs)


def passed_along(value, axis, steps):
    count = lax.axis_size(axis)
    leading, last = (max(0, -steps), min(count, count - steps))
    return lax.ppermute(value, axis, [(source, source + steps) for source in range(leading, last)])


def kernel_block(target_geo, source_geo, offset):
    delta_x = target_geo[0][:, None] - source_geo[0][None, :] + spacing * offset
    delta_y = target_geo[1][:, None] - source_geo[1][None, :]
    delta_z = target_geo[2][:, None] - source_geo[2][None, :]
    square = delta_x * delta_x + delta_y * delta_y + delta_z * delta_z
    return target_geo[3][:, None] * source_geo[3][None, :] * (soften / (soften + square))


def high_product(left_matrix, right_matrix):
    return jnp.dot(left_matrix, right_matrix.astype(jnp.float32), precision=lax.Precision.HIGHEST)


def high_transposed(left_matrix, right_matrix):
    return lax.dot_general(
        left_matrix,
        right_matrix.astype(jnp.float32),
        (((1,), (1,)), ((), ())),
        precision=lax.Precision.HIGHEST,
    )


def per_device(
    light,
    probes,
    near_list,
    far_list,
    leaf_basis,
    leaf_transfer,
    far_coupling,
    up_transfer,
    upper_coupling,
):
    leaf_count = leaf_basis.shape[0]
    leaf_size = leaf_basis.shape[1]
    rank_size = leaf_basis.shape[2]
    light_rows = light.shape[0]
    device_index = lax.axis_index(("leaf", "sub"))
    anchor = device_index * leaf_count
    stacked = jnp.concatenate([light, probes], axis=0)
    padded = extended(stacked, ((("leaf", "sub"), 1),), HALO * leaf_size)
    local_ids = anchor + jnp.arange(leaf_count, dtype=jnp.int32)
    target_geo = probes.astype(jnp.float32).reshape(4, leaf_count, leaf_size)
    tile_maker = jax.vmap(kernel_block, in_axes=(1, 1, None))
    near_terms = jnp.zeros((light_rows, leaf_count, leaf_size), jnp.float32)
    for step in range(-HALO, HALO + 1):
        start = (HALO + step) * leaf_size
        window = padded[:, start : start + leaf_count * leaf_size]
        source_values = window[:light_rows].reshape(light_rows, leaf_count, leaf_size)
        source_geo = window[light_rows:].astype(jnp.float32).reshape(4, leaf_count, leaf_size)
        kernel_tiles = tile_maker(target_geo, source_geo, jnp.float32(-step)).astype(jnp.bfloat16)
        contribution = jnp.einsum(
            "rjl,jil->rji", source_values, kernel_tiles, preferred_element_type=jnp.float32
        )
        if step == 0:
            near_terms = near_terms + contribution
        else:
            chosen = jnp.any(near_list == (local_ids + step)[:, None], axis=1).astype(jnp.float32)
            near_terms = near_terms + contribution * chosen[None, :, None]
    light_blocks = light.reshape(light_rows, leaf_count, leaf_size)
    coefficients = jnp.einsum(
        "rjl,jlk->jrk", light_blocks, leaf_basis, preferred_element_type=jnp.float32
    ).astype(jnp.bfloat16)
    coeff_flat = coefficients.reshape(leaf_count, light_rows * rank_size)
    entries = far_list.reshape(-1)
    groups = lax.axis_size("sub")
    peer_row = entries // leaf_count // groups
    which_leaf = entries % leaf_count
    pooled = lax.all_gather(coeff_flat, "leaf", axis=0, tiled=True)
    picked = pooled[peer_row * leaf_count + which_leaf]
    picked = picked.reshape(leaf_count, -1, light_rows, rank_size)
    far_terms = jnp.einsum(
        "jcrk,jckm->jrm", picked, far_coupling, preferred_element_type=jnp.float32
    )
    upward = [
        jnp.einsum("jrk,jkm->rm", coefficients, leaf_transfer, preferred_element_type=jnp.float32)
    ]
    for height in range(UPLV):
        parity = device_index >> height & 1
        mine_term = high_product(upward[-1], up_transfer[height][parity])
        other_term = from_partner(mine_term, ("leaf", "sub"), height)
        left_term = jnp.where(parity == 0, mine_term, other_term)
        right_term = jnp.where(parity == 0, other_term, mine_term)
        upward.append(left_term + right_term)
    downward = None
    for height in range(UPLV, -1, -1):
        stride = 2 ** (height + 1)
        lower_part = passed_along(upward[height], ("leaf", "sub"), stride)
        upper_part = passed_along(upward[height], ("leaf", "sub"), -stride)
        coupled = high_product(lower_part, upper_coupling[height, 0]) + high_product(
            upper_part, upper_coupling[height, 1]
        )
        if downward is not None:
            parity = device_index >> height & 1
            coupled = coupled + high_transposed(downward, up_transfer[height][parity])
        downward = coupled
    pulled = jnp.einsum(
        "rk,jmk->jrm", downward, leaf_transfer.astype(jnp.float32), precision=lax.Precision.HIGHEST
    )
    leaf_far = (far_terms + pulled).astype(jnp.bfloat16)
    spread = jnp.einsum("jrk,jlk->rjl", leaf_far, leaf_basis, preferred_element_type=jnp.float32)
    combined = near_terms + spread
    return combined.reshape(light_rows, leaf_count * leaf_size).astype(jnp.bfloat16)


def solution(mesh):
    return jax.shard_map(
        per_device,
        mesh=mesh,
        in_specs=(
            P(None, ("leaf", "sub")),
            P(None, ("leaf", "sub")),
            P(("leaf", "sub"), None),
            P(("leaf", "sub"), None),
            P(("leaf", "sub"), None, None),
            P(("leaf", "sub"), None, None),
            P(("leaf", "sub"), None, None, None),
            P(),
            P(),
        ),
        out_specs=P(None, ("leaf", "sub")),
        check_vma=False,
    )
```

profile of v0, /device:TPU:1, one launch (start us, length us, event | category | flops | bytes accessed | tf_op | source)
XLA Modules:
  0.0 131.3 jit_solution(11800955980936551876)
XLA Ops:
  6.5 0.9 copy-done
  7.5 1.1 convolution_convert_fusion
  8.6 1.1 convolution_bitcast_fusion.3
  9.7 6.0 %collective-permute-start.3 = (f32[32,64]{1,0:T(8,128)S(1)}, f32[32,64]{1,0:T(8,128)S(1)}, u32[]{:S(2)}, u32[]{:S(2)}) collective-permute-start(f32[32,64]{1,0:T(8,128)S(1)} %convolution_bitcast_fusion.3), channel_id=1, source_target_pairs={{2,0},{3,1},{4,2},{5,3},{6,4},{7,5},{8,6},{9,7},{10,8},{11,9},{12,... | collective-permute-start | bytes 24584 | tf_op jit(solution)/shard_map/ppermute | solution.py:34
  15.7 1.9 %collective-permute-start.2 = (f32[32,64]{1,0:T(8,128)S(1)}, f32[32,64]{1,0:T(8,128)S(1)}, u32[]{:S(2)}, u32[]{:S(2)}) collective-permute-start(f32[32,64]{1,0:T(8,128)S(1)} %convolution_bitcast_fusion.3), channel_id=1, source_target_pairs={{0,2},{1,3},{2,4},{3,5},{4,6},{5,7},{6,8},{7,9},{8,10},{9,11},{10,... | collective-permute-start | bytes 24584 | tf_op jit(solution)/shard_map/ppermute | solution.py:34
  17.7 0.8 fusion.206
  18.6 2.8 %collective-permute-start.4 = (f32[32,64]{1,0:T(8,128)S(1)}, f32[32,64]{1,0:T(8,128)S(1)}, u32[]{:S(2)}, u32[]{:S(2)}) collective-permute-start(f32[32,64]{1,0:T(8,128)S(1)} %fusion.154), channel_id=1, source_target_pairs={{0,1},{1,0},{2,3},{3,2},{4,5},{5,4},{6,7},{7,6},{8,9},{9,8},{10,11... | collective-permute-start | bytes 24584 | tf_op jit(solution)/shard_map/ppermute | solution.py:28
  21.4 0.7 reshape.385
  22.2 0.9 constant_dynamic-update-slice_fusion.1
  23.1 0.8 fusion.207
  23.9 2.5 %collective-permute-start = (bf16[36,1024]{1,0:T(8,128)(2,1)S(1)}, bf16[36,1024]{1,0:T(8,128)(2,1)S(1)}, u32[]{:S(2)}, u32[]{:S(2)}) collective-permute-start(bf16[36,1024]{1,0:T(8,128)(2,1)S(1)} %get-tuple-element.74), channel_id=1, source_target_pairs={{0,1},{1,2},{2,3},{3,4},{4,5},{5,6},{6,7},{7,8},{8,9},{9,10},{10,1... | collective-permute-start | bytes 221192 | tf_op jit(solution)/shard_map/ppermute | solution.py:19
  26.4 6.9 %collective-permute-start.1 = (bf16[36,1024]{1,0:T(8,128)(2,1)S(1)}, bf16[36,1024]{1,0:T(8,128)(2,1)S(1)}, u32[]{:S(2)}, u32[]{:S(2)}) collective-permute-start(bf16[36,1024]{1,0:T(8,128)(2,1)S(1)} %get-tuple-element.73), channel_id=1, source_target_pairs={{1,0},{2,1},{3,2},{4,3},{5,4},{6,5},{7,6},{8,7},{9,8},{10,9},{11,1... | collective-permute-start | bytes 221192 | tf_op jit(solution)/shard_map/ppermute | solution.py:20
  33.4 0.8 reshape.386
  34.3 0.7 compare_reduce_fusion
  35.2 3.1 %collective-permute-start.6 = (f32[32,64]{1,0:T(8,128)S(1)}, f32[32,64]{1,0:T(8,128)S(1)}, u32[]{:S(2)}, u32[]{:S(2)}) collective-permute-start(f32[32,64]{1,0:T(8,128)S(1)} %select_add_fusion.2), channel_id=1, source_target_pairs={{4,0},{5,1},{6,2},{7,3},{8,4},{9,5},{10,6},{11,7},{12,8},{13,9},{1... | collective-permute-start | bytes 24584 | tf_op jit(solution)/shard_map/ppermute | solution.py:34
  38.5 4.3 %collective-permute-start.7 = (f32[32,64]{1,0:T(8,128)S(1)}, f32[32,64]{1,0:T(8,128)S(1)}, u32[]{:S(2)}, u32[]{:S(2)}) collective-permute-start(f32[32,64]{1,0:T(8,128)S(1)} %fusion.147), channel_id=1, source_target_pairs={{0,2},{1,3},{2,0},{3,1},{4,6},{5,7},{6,4},{7,5},{8,10},{9,11},{10,... | collective-permute-start | bytes 24584 | tf_op jit(solution)/shard_map/ppermute | solution.py:28
  42.9 1.7 %collective-permute-done.7 = f32[32,64]{1,0:T(8,128)S(1)} collective-permute-done((f32[32,64]{1,0:T(8,128)S(1)}, f32[32,64]{1,0:T(8,128)S(1)}, u32[]{:S(2)}, u32[]{:S(2)}) %collective-permute-start.7) | collective-permute-done | bytes 8224 | tf_op jit(solution)/shard_map/ppermute | solution.py:28
  44.6 3.4 %collective-permute-start.5 = (f32[32,64]{1,0:T(8,128)S(1)}, f32[32,64]{1,0:T(8,128)S(1)}, u32[]{:S(2)}, u32[]{:S(2)}) collective-permute-start(f32[32,64]{1,0:T(8,128)S(1)} %select_add_fusion.2), channel_id=1, source_target_pairs={{0,4},{1,5},{2,6},{3,7},{4,8},{5,9},{6,10},{7,11},{8,12},{9,13},{1... | collective-permute-start | bytes 24584 | tf_op jit(solution)/shard_map/ppermute | solution.py:34
  48.2 1.9 %collective-permute-start.10 = (f32[32,64]{1,0:T(8,128)S(1)}, f32[32,64]{1,0:T(8,128)S(1)}, u32[]{:S(2)}, u32[]{:S(2)}) collective-permute-start(f32[32,64]{1,0:T(8,128)S(1)} %fusion.140), channel_id=1, source_target_pairs={{0,4},{1,5},{2,6},{3,7},{4,0},{5,1},{6,2},{7,3},{8,12},{9,13},{10,... | collective-permute-start | bytes 24584 | tf_op jit(solution)/shard_map/ppermute | solution.py:28
  50.2 1.0 collective-permute-done.10
  51.3 1.3 collective-permute-start.9
  52.6 3.6 %collective-permute-done.9 = f32[32,64]{1,0:T(8,128)S(1)} collective-permute-done((f32[32,64]{1,0:T(8,128)S(1)}, f32[32,64]{1,0:T(8,128)S(1)}, u32[]{:S(2)}, u32[]{:S(2)}) %collective-permute-start.9) | collective-permute-done | bytes 8224 | tf_op jit(solution)/shard_map/ppermute | solution.py:34
  56.2 1.3 collective-permute-start.12
  57.6 5.8 %collective-permute-done.12 = f32[32,64]{1,0:T(8,128)S(1)} collective-permute-done((f32[32,64]{1,0:T(8,128)S(1)}, f32[32,64]{1,0:T(8,128)S(1)}, u32[]{:S(2)}, u32[]{:S(2)}) %collective-permute-start.12) | collective-permute-done | bytes 8224 | tf_op jit(solution)/shard_map/ppermute | solution.py:34
  63.4 5.1 %collective-permute-start.11 = (f32[32,64]{1,0:T(8,128)S(1)}, f32[32,64]{1,0:T(8,128)S(1)}, u32[]{:S(2)}, u32[]{:S(2)}) collective-permute-start(f32[32,64]{1,0:T(8,128)S(1)} %select_add_fusion), channel_id=1, source_target_pairs={{0,16},{1,17},{2,18},{3,19},{4,20},{5,21},{6,22},{7,23},{8,24},{9,... | collective-permute-start | bytes 24584 | tf_op jit(solution)/shard_map/ppermute | solution.py:34
  68.5 0.7 collective-permute-done.11
  69.3 4.5 %collective-permute-start.8 = (f32[32,64]{1,0:T(8,128)S(1)}, f32[32,64]{1,0:T(8,128)S(1)}, u32[]{:S(2)}, u32[]{:S(2)}) collective-permute-start(f32[32,64]{1,0:T(8,128)S(1)} %select_add_fusion.1), channel_id=1, source_target_pairs={{0,8},{1,9},{2,10},{3,11},{4,12},{5,13},{6,14},{7,15},{8,16},{9,17... | collective-permute-start | bytes 24584 | tf_op jit(solution)/shard_map/ppermute | solution.py:34
  74.0 0.6 collective-permute-done.8
  75.5 0.2 slice_reduce_fusion.27
  75.7 0.2 slice_reduce_fusion.19
  76.0 0.2 slice_reduce_fusion.11
  76.3 0.2 slice_reduce_fusion.3
  76.6 2.7 %convolution_multiply_fusion.7 = f32[8,256,32]{1,2,0:T(8,128)S(1)} fusion(f32[8,256]{1,0:T(8,128)S(1)} %sub.188, f32[8,256]{1,0:T(8,128)S(1)} %sub.186, f32[8,256]{1,0:T(8,128)S(1)} %sub.183, f32[8,256]{1,0:T(8,128)S(1)} %sub.181, f32[8,256]{1,0:T(8,128)S(1)} %sub.178, f32[8,256]{1,0:T(8,128)S(1)} %sub.176, f32[8,256]{1,0:T(8,128)S(1)} %mul.326, ...), kind=kOutput, calls=%fused_computation.28 | convolution fusion | flops 40960000 | bytes 458784 | tf_op jit(solution)/shard_map/rjl,jil->rji/dot_general | solution.py:87
  79.3 2.6 %fusion.8 = f32[8,256,32]{1,2,0:T(8,128)S(1)} fusion(f32[8,256,32]{1,2,0:T(8,128)S(1)} %convolution_multiply_fusion.7, f32[8,256]{1,0:T(8,128)S(1)} %sub.388, f32[8,256]{1,0:T(8,128)S(1)} %sub.385, f32[8,256]{1,0:T(8,128)S(1)} %sub.382, f32[8,256]{1,0:T(8,128)S(1)} %mul.337, f32[8,256]{1,0:T(8,128)S(1)} %sub.186, f32[8,256]{1,0:T(8,128)S(1)} %sub.181, ...), kind=kOutput, calls=%fused_computation.27 | convolution fusion | flops 41025536 | bytes 720928 | tf_op jit(solution)/shard_map/rjl,jil->rji/dot_general | solution.py:87
  81.9 2.7 %fusion.7 = f32[8,256,32]{1,2,0:T(8,128)S(1)} fusion(f32[8,256,32]{1,2,0:T(8,128)S(1)} %fusion.8, f32[8,256]{1,0:T(8,128)S(1)} %sub.397, f32[8,256]{1,0:T(8,128)S(1)} %sub.394, f32[8,256]{1,0:T(8,128)S(1)} %sub.391, f32[8,256]{1,0:T(8,128)S(1)} %mul.346, f32[8,256]{1,0:T(8,128)S(1)} %sub.186, f32[8,256]{1,0:T(8,128)S(1)} %sub.181, f32[8,256]{1,0:T(8,128)S(1)} %sub.176, ...), kind=kOutput, calls=%fused_computation.25 | convolution fusion | flops 41025536 | bytes 720928 | tf_op jit(solution)/shard_map/rjl,jil->rji/dot_general | solution.py:87
  84.6 2.6 %fusion.6 = f32[8,256,32]{1,2,0:T(8,128)S(1)} fusion(f32[8,256,32]{1,2,0:T(8,128)S(1)} %fusion.7, f32[8,256]{1,0:T(8,128)S(1)} %sub.406, f32[8,256]{1,0:T(8,128)S(1)} %sub.403, f32[8,256]{1,0:T(8,128)S(1)} %sub.400, f32[8,256]{1,0:T(8,128)S(1)} %mul.355, f32[8,256]{1,0:T(8,128)S(1)} %sub.186, f32[8,256]{1,0:T(8,128)S(1)} %sub.181, f32[8,256]{1,0:T(8,128)S(1)} %sub.176, ...), kind=kOutput, calls=%fused_computation.23 | convolution fusion | flops 41025536 | bytes 720928 | tf_op jit(solution)/shard_map/rjl,jil->rji/dot_general | solution.py:87
  87.2 2.6 %convolution_add_fusion = f32[8,256,32]{1,2,0:T(8,128)S(1)} fusion(f32[8,256,32]{1,2,0:T(8,128)S(1)} %fusion.6, f32[8,256]{1,0:T(8,128)S(1)} %sub.186, f32[8,256]{1,0:T(8,128)S(1)} %sub.181, f32[8,256]{1,0:T(8,128)S(1)} %sub.176, f32[8,256]{1,0:T(8,128)S(1)} %mul.324, bf16[4,8,8,256]{3,2,1,0:T(8,128)(2,1)S(1)} %bitcast.128), kind=kOutput, calls=%fused_computation.21 | convolution fusion | flops 40435712 | bytes 688128 | tf_op jit(solution)/shard_map/rjl,jil->rji/dot_general | solution.py:87
  89.9 2.6 %fusion.5 = f32[8,256,32]{1,2,0:T(8,128)S(1)} fusion(f32[8,256,32]{1,2,0:T(8,128)S(1)} %convolution_add_fusion, f32[8,256]{1,0:T(8,128)S(1)} %sub.421, f32[8,256]{1,0:T(8,128)S(1)} %sub.418, f32[8,256]{1,0:T(8,128)S(1)} %sub.415, f32[8,256]{1,0:T(8,128)S(1)} %mul.370, f32[8,256]{1,0:T(8,128)S(1)} %sub.186, f32[8,256]{1,0:T(8,128)S(1)} %sub.181, ...), kind=kOutput, calls=%fused_computation.20 | convolution fusion | flops 41025536 | bytes 720928 | tf_op jit(solution)/shard_map/rjl,jil->rji/dot_general | solution.py:87
  92.5 2.6 %fusion.4 = f32[8,256,32]{1,2,0:T(8,128)S(1)} fusion(f32[8,256,32]{1,2,0:T(8,128)S(1)} %fusion.5, f32[8,256]{1,0:T(8,128)S(1)} %sub.430, f32[8,256]{1,0:T(8,128)S(1)} %sub.427, f32[8,256]{1,0:T(8,128)S(1)} %sub.424, f32[8,256]{1,0:T(8,128)S(1)} %mul.380, f32[8,256]{1,0:T(8,128)S(1)} %sub.186, f32[8,256]{1,0:T(8,128)S(1)} %sub.181, f32[8,256]{1,0:T(8,128)S(1)} %sub.176, ...), kind=kOutput, calls=%fused_computation.18 | convolution fusion | flops 41025536 | bytes 720928 | tf_op jit(solution)/shard_map/rjl,jil->rji/dot_general | solution.py:87
  95.1 2.6 %fusion.3 = f32[8,256,32]{1,2,0:T(8,128)S(1)} fusion(f32[8,256,32]{1,2,0:T(8,128)S(1)} %fusion.4, f32[8,256]{1,0:T(8,128)S(1)} %sub.439, f32[8,256]{1,0:T(8,128)S(1)} %sub.436, f32[8,256]{1,0:T(8,128)S(1)} %sub.433, f32[8,256]{1,0:T(8,128)S(1)} %mul.390, f32[8,256]{1,0:T(8,128)S(1)} %sub.186, f32[8,256]{1,0:T(8,128)S(1)} %sub.181, f32[8,256]{1,0:T(8,128)S(1)} %sub.176, ...), kind=kOutput, calls=%fused_computation.16 | convolution fusion | flops 41025536 | bytes 720928 | tf_op jit(solution)/shard_map/rjl,jil->rji/dot_general | solution.py:87
  97.8 2.7 %fusion.2 = f32[32,8,256]{2,0,1:T(8,128)} fusion(f32[8,256,32]{1,2,0:T(8,128)S(1)} %fusion.3, f32[8,256]{1,0:T(8,128)S(1)} %sub.448, f32[8,256]{1,0:T(8,128)S(1)} %sub.445, f32[8,256]{1,0:T(8,128)S(1)} %sub.442, f32[8,256]{1,0:T(8,128)S(1)} %mul.400, f32[8,256]{1,0:T(8,128)S(1)} %sub.186, f32[8,256]{1,0:T(8,128)S(1)} %sub.181, f32[8,256]{1,0:T(8,128)S(1)} %sub.176, ...), kind=kOutput, calls=%fused_computation.14 | convolution fusion | flops 41025536 | bytes 720928 | tf_op jit(solution)/shard_map/rjl,jil->rji/dot_general | solution.py:87
  100.5 12.3 %all-gather.2.cloned.1.call-done = bf16[1024,2048]{1,0:T(8,128)(2,1)} async-done(((bf16[8,2048]{1,0:T(8,128)(2,1)}), bf16[1024,2048]{1,0:T(8,128)(2,1)}) %all-gather.2.cloned.1.call-update) | async-done | bytes 4194320 | tf_op jit(solution)/shard_map/all_gather | solution.py:104
  112.8 5.1 %gather_fusion = bf16[256,2048]{1,0:T(8,128)(2,1)S(1)} fusion(bf16[1024,2048]{1,0:T(8,128)(2,1)} %all-gather.2.cloned.1.call-done, s32[1024]{0:T(1024)S(1)} %pad_clamp_fusion), kind=kCustom, calls=%fused_computation | custom fusion | bytes 2098176 | tf_op jit(solution)/shard_map/gather | solution.py:105
  117.9 2.2 %reshape.387 = bf16[8,32,32,64]{3,2,1,0:T(8,128)(2,1)S(1)} reshape(bf16[256,2048]{1,0:T(8,128)(2,1)S(1)} %gather_fusion) | data formatting | bytes 2097152 | tf_op jit(solution)/shard_map/reshape | solution.py:106
  120.1 3.0 %convolution_bitcast_fusion.1 = f32[8,32,64]{2,1,0:T(8,128)S(1)} fusion(bf16[8,32,32,64]{3,2,1,0:T(8,128)(2,1)S(1)} %reshape.387, bf16[8,32,64,64]{3,2,1,0:T(8,128)(2,1)} %param.15), kind=kOutput, calls=%fused_computation.31 | convolution fusion | flops 67108864 | bytes 3211264 | tf_op jit(solution)/shard_map/jcrk,jckm->jrm/dot_general | solution.py:107
  123.1 0.5 fusion.12
  123.6 0.2 fusion.10
  123.8 0.7 copy.33
  (89 shorter events, 2.4 us)
Async XLA Ops:
  6.5 1.0 copy-start
  6.5 36.3 %copy-start.4 = (bf16[4,2,64,64]{3,2,1,0:T(8,128)(2,1)S(1)}, bf16[4,2,64,64]{3,2,1,0:T(8,128)(2,1)}, u32[]{:S(2)}) copy-start(bf16[4,2,64,64]{3,2,1,0:T(8,128)(2,1)} %param.17) | copy-start | bytes 196612
  6.5 106.2 %all-gather.2.cloned.1.call-start = ((), (), s32[]{:S(2)}) async-start(), calls=%async_computation | async-start | bytes 4227072 | tf_op jit(solution)/shard_map/all_gather | solution.py:104
  9.7 28.8 %collective-permute-start.3 = (f32[32,64]{1,0:T(8,128)S(1)}, f32[32,64]{1,0:T(8,128)S(1)}, u32[]{:S(2)}, u32[]{:S(2)}) collective-permute-start(f32[32,64]{1,0:T(8,128)S(1)} %convolution_bitcast_fusion.3), channel_id=1, source_target_pairs={{2,0},{3,1},{4,2},{5,3},{6,4},{7,5},{8,6},{9,7},{10,8},{11,9},{12,... | collective-permute-start | bytes 24584 | tf_op jit(solution)/shard_map/ppermute | solution.py:34
  15.7 59.5 %collective-permute-start.2 = (f32[32,64]{1,0:T(8,128)S(1)}, f32[32,64]{1,0:T(8,128)S(1)}, u32[]{:S(2)}, u32[]{:S(2)}) collective-permute-start(f32[32,64]{1,0:T(8,128)S(1)} %convolution_bitcast_fusion.3), channel_id=1, source_target_pairs={{0,2},{1,3},{2,4},{3,5},{4,6},{5,7},{6,8},{7,9},{8,10},{9,11},{10,... | collective-permute-start | bytes 24584 | tf_op jit(solution)/shard_map/ppermute | solution.py:34
  18.6 16.5 %collective-permute-start.4 = (f32[32,64]{1,0:T(8,128)S(1)}, f32[32,64]{1,0:T(8,128)S(1)}, u32[]{:S(2)}, u32[]{:S(2)}) collective-permute-start(f32[32,64]{1,0:T(8,128)S(1)} %fusion.154), channel_id=1, source_target_pairs={{0,1},{1,0},{2,3},{3,2},{4,5},{5,4},{6,7},{7,6},{8,9},{9,8},{10,11... | collective-permute-start | bytes 24584 | tf_op jit(solution)/shard_map/ppermute | solution.py:28
  23.9 51.5 %collective-permute-start = (bf16[36,1024]{1,0:T(8,128)(2,1)S(1)}, bf16[36,1024]{1,0:T(8,128)(2,1)S(1)}, u32[]{:S(2)}, u32[]{:S(2)}) collective-permute-start(bf16[36,1024]{1,0:T(8,128)(2,1)S(1)} %get-tuple-element.74), channel_id=1, source_target_pairs={{0,1},{1,2},{2,3},{3,4},{4,5},{5,6},{6,7},{7,8},{8,9},{9,10},{10,1... | collective-permute-start | bytes 221192 | tf_op jit(solution)/shard_map/ppermute | solution.py:19
  26.4 49.0 %collective-permute-start.1 = (bf16[36,1024]{1,0:T(8,128)(2,1)S(1)}, bf16[36,1024]{1,0:T(8,128)(2,1)S(1)}, u32[]{:S(2)}, u32[]{:S(2)}) collective-permute-start(bf16[36,1024]{1,0:T(8,128)(2,1)S(1)} %get-tuple-element.73), channel_id=1, source_target_pairs={{1,0},{2,1},{3,2},{4,3},{5,4},{6,5},{7,6},{8,7},{9,8},{10,9},{11,1... | collective-permute-start | bytes 221192 | tf_op jit(solution)/shard_map/ppermute | solution.py:20
  35.2 13.0 %collective-permute-start.6 = (f32[32,64]{1,0:T(8,128)S(1)}, f32[32,64]{1,0:T(8,128)S(1)}, u32[]{:S(2)}, u32[]{:S(2)}) collective-permute-start(f32[32,64]{1,0:T(8,128)S(1)} %select_add_fusion.2), channel_id=1, source_target_pairs={{4,0},{5,1},{6,2},{7,3},{8,4},{9,5},{10,6},{11,7},{12,8},{13,9},{1... | collective-permute-start | bytes 24584 | tf_op jit(solution)/shard_map/ppermute | solution.py:34
  38.5 6.1 %collective-permute-start.7 = (f32[32,64]{1,0:T(8,128)S(1)}, f32[32,64]{1,0:T(8,128)S(1)}, u32[]{:S(2)}, u32[]{:S(2)}) collective-permute-start(f32[32,64]{1,0:T(8,128)S(1)} %fusion.147), channel_id=1, source_target_pairs={{0,2},{1,3},{2,0},{3,1},{4,6},{5,7},{6,4},{7,5},{8,10},{9,11},{10,... | collective-permute-start | bytes 24584 | tf_op jit(solution)/shard_map/ppermute | solution.py:28
  44.6 30.3 %collective-permute-start.5 = (f32[32,64]{1,0:T(8,128)S(1)}, f32[32,64]{1,0:T(8,128)S(1)}, u32[]{:S(2)}, u32[]{:S(2)}) collective-permute-start(f32[32,64]{1,0:T(8,128)S(1)} %select_add_fusion.2), channel_id=1, source_target_pairs={{0,4},{1,5},{2,6},{3,7},{4,8},{5,9},{6,10},{7,11},{8,12},{9,13},{1... | collective-permute-start | bytes 24584 | tf_op jit(solution)/shard_map/ppermute | solution.py:34
  48.2 3.1 %collective-permute-start.10 = (f32[32,64]{1,0:T(8,128)S(1)}, f32[32,64]{1,0:T(8,128)S(1)}, u32[]{:S(2)}, u32[]{:S(2)}) collective-permute-start(f32[32,64]{1,0:T(8,128)S(1)} %fusion.140), channel_id=1, source_target_pairs={{0,4},{1,5},{2,6},{3,7},{4,0},{5,1},{6,2},{7,3},{8,12},{9,13},{10,... | collective-permute-start | bytes 24584 | tf_op jit(solution)/shard_map/ppermute | solution.py:28
  51.3 4.9 %collective-permute-start.9 = (f32[32,64]{1,0:T(8,128)S(1)}, f32[32,64]{1,0:T(8,128)S(1)}, u32[]{:S(2)}, u32[]{:S(2)}) collective-permute-start(f32[32,64]{1,0:T(8,128)S(1)} %select_add_fusion.1), channel_id=1, source_target_pairs={{8,0},{9,1},{10,2},{11,3},{12,4},{13,5},{14,6},{15,7},{16,8},{17,9... | collective-permute-start | bytes 24584 | tf_op jit(solution)/shard_map/ppermute | solution.py:34
  56.2 7.2 %collective-permute-start.12 = (f32[32,64]{1,0:T(8,128)S(1)}, f32[32,64]{1,0:T(8,128)S(1)}, u32[]{:S(2)}, u32[]{:S(2)}) collective-permute-start(f32[32,64]{1,0:T(8,128)S(1)} %select_add_fusion), channel_id=1, source_target_pairs={{16,0},{17,1},{18,2},{19,3},{20,4},{21,5},{22,6},{23,7},{24,8},{25... | collective-permute-start | bytes 24584 | tf_op jit(solution)/shard_map/ppermute | solution.py:34
  63.4 5.9 %collective-permute-start.11 = (f32[32,64]{1,0:T(8,128)S(1)}, f32[32,64]{1,0:T(8,128)S(1)}, u32[]{:S(2)}, u32[]{:S(2)}) collective-permute-start(f32[32,64]{1,0:T(8,128)S(1)} %select_add_fusion), channel_id=1, source_target_pairs={{0,16},{1,17},{2,18},{3,19},{4,20},{5,21},{6,22},{7,23},{8,24},{9,... | collective-permute-start | bytes 24584 | tf_op jit(solution)/shard_map/ppermute | solution.py:34
  69.3 5.4 %collective-permute-start.8 = (f32[32,64]{1,0:T(8,128)S(1)}, f32[32,64]{1,0:T(8,128)S(1)}, u32[]{:S(2)}, u32[]{:S(2)}) collective-permute-start(f32[32,64]{1,0:T(8,128)S(1)} %select_add_fusion.1), channel_id=1, source_target_pairs={{0,8},{1,9},{2,10},{3,11},{4,12},{5,13},{6,14},{7,15},{8,16},{9,17... | collective-permute-start | bytes 24584 | tf_op jit(solution)/shard_map/ppermute | solution.py:34
  84.6 2.6 %copy-start.1 = (bf16[32,2048]{1,0:T(8,128)(2,1)S(1)}, bf16[32,2048]{1,0:T(8,128)(2,1)}, u32[]{:S(2)}) copy-start(bf16[32,2048]{1,0:T(8,128)(2,1)} %param.9) | copy-start | bytes 393220
  120.1 3.1 %copy-start.2 = (bf16[8,64,64]{2,1,0:T(8,128)(2,1)S(1)}, bf16[8,64,64]{2,1,0:T(8,128)(2,1)}, u32[]{:S(2)}) copy-start(bf16[8,64,64]{2,1,0:T(8,128)(2,1)} %param.14) | copy-start | bytes 196612
  120.1 3.5 %copy-start.3 = (f32[32,8,256]{2,0,1:T(8,128)S(1)}, f32[32,8,256]{2,0,1:T(8,128)}, u32[]{:S(2)}) copy-start(f32[32,8,256]{2,0,1:T(8,128)} %fusion.2) | copy-start | bytes 786436
Sparse Core Ops, SparseCore 0:
  22.3 90.4 all-gather.1
where the time goes:
time: 132 us; the launch traced here: 131 us
  starting transfers between devices  45.1 us (34%)
  matrix products  31.5 us (24%)
  waiting for transfers between devices  25.8 us (20%)
  between operations  14.2 us (11%)
  local copies, waits for them, and re-layouts  13.1 us (10%)
  other arithmetic  1.75 us (1%)
    ppermute x8, starting transfers between devices, passed_along(): lax.ppermute(value, axis, [(source, source + steps) for source in range(l...  26.6 us
    dot_general x9, matrix products, per_device(): jnp.einsum('rjl,jil->rji', source_values, kernel_tiles, preferred_element...  23.8 us
    all_gather x1, waiting for transfers between devices, per_device(): pooled = lax.all_gather(coeff_flat, 'leaf', axis=0, tiled=True)  12.3 us
    ppermute x8, waiting for transfers between devices, passed_along(): lax.ppermute(value, axis, [(source, source + steps) for source in range(l...  10.8 us
    ppermute x3, starting transfers between devices, from_partner(): return lax.ppermute(value, axis, pairs)  9.02 us
    ppermute x1, starting transfers between devices, extended(): after = lax.ppermute(leading, axis, down)  6.9 us
    gather x1, local copies, waits for them, and re-layouts, per_device(): picked = pooled[peer_row * leaf_count + which_leaf]  5.09 us
    dot_general x1, matrix products, per_device(): jnp.einsum('jcrk,jckm->jrm', picked, far_coupling, preferred_element_type...  3.03 us
  transfers between devices with their start and end apart: 14, of which 7 were waited for; matrix products, arithmetic and copies ran while one was open for 24% of the time, Pallas kernels for 0%

commit v1 on v0

--- a/solution.py
+++ b/solution.py
@@ -101,7 +101,9 @@
     groups = lax.axis_size("sub")
     peer_row = entries // leaf_count // groups
     which_leaf = entries % leaf_count
-    pooled = lax.all_gather(coeff_flat, "leaf", axis=0, tiled=True)
+    pooled = jnp.concatenate(
+        lax.all_to_all(jnp.stack([coeff_flat] * lax.axis_size("leaf")), "leaf", 0, 0), axis=0
+    )
     picked = pooled[peer_row * leaf_count + which_leaf]
     picked = picked.reshape(leaf_count, -1, light_rows, rank_size)
     far_terms = jnp.einsum(

time: 132 us -> 204 us (1.55)
  the two profiles are of different devices: /device:TPU:1 before, /device:TPU:256 now
where the time goes in v1:
time: 204 us; the launch traced here: 203 us
  waiting for transfers between devices  89.2 us (44%)
  starting transfers between devices  68.3 us (33%)
  matrix products  31.5 us (15%)
  local copies, waits for them, and re-layouts  13.4 us (7%)
    ppermute x8, waiting for transfers between devices, passed_along(): lax.ppermute(value, axis, [(source, source + steps) for source in range(l...  83.4 us
    ppermute x8, starting transfers between devices, passed_along(): lax.ppermute(value, axis, [(source, source + steps) for source in range(l...  31.5 us
    dot_general x9, matrix products, per_device(): jnp.einsum('rjl,jil->rji', source_values, kernel_tiles, preferred_element...  23.8 us
    all_to_all x1, starting transfers between devices, per_device(): lax.all_to_all(jnp.stack([coeff_flat] * lax.axis_size('leaf')), 'leaf', 0...  14.7 us
    ppermute x3, starting transfers between devices, from_partner(): return lax.ppermute(value, axis, pairs)  11 us
    ppermute x1, starting transfers between devices, extended(): after = lax.ppermute(leading, axis, down)  8.55 us
    ppermute x3, waiting for transfers between devices, from_partner(): return lax.ppermute(value, axis, pairs)  5.77 us
    gather x1, local copies, waits for them, and re-layouts, per_device(): picked = pooled[peer_row * leaf_count + which_leaf]  5.09 us
  transfers between devices with their start and end apart: 14, of which 7 were waited for; matrix products, arithmetic and copies ran while one was open for 15% of the time, Pallas kernels for 0%

profile of v1, /device:TPU:256, one launch (start us, length us, event | category | flops | bytes accessed | tf_op | source)
XLA Modules:
  0.0 203.4 jit_solution(7602880766279877615)
XLA Ops:
  0.0 0.9 copy-done
  1.0 1.1 convolution_convert_fusion
  2.0 1.1 convolution_bitcast_fusion.3
  3.2 6.4 %collective-permute-start.3 = (f32[32,64]{1,0:T(8,128)S(1)}, f32[32,64]{1,0:T(8,128)S(1)}, u32[]{:S(2)}, u32[]{:S(2)}) collective-permute-start(f32[32,64]{1,0:T(8,128)S(1)} %convolution_bitcast_fusion.3), channel_id=1, source_target_pairs={{2,0},{3,1},{4,2},{5,3},{6,4},{7,5},{8,6},{9,7},{10,8},{11,9},{12,... | collective-permute-start | bytes 24584 | tf_op jit(solution)/shard_map/ppermute | solution.py:34
  9.5 1.9 collective-permute-start.2
  11.5 0.8 fusion.206
  12.4 2.5 %collective-permute-start.4 = (f32[32,64]{1,0:T(8,128)S(1)}, f32[32,64]{1,0:T(8,128)S(1)}, u32[]{:S(2)}, u32[]{:S(2)}) collective-permute-start(f32[32,64]{1,0:T(8,128)S(1)} %fusion.154), channel_id=1, source_target_pairs={{0,1},{1,0},{2,3},{3,2},{4,5},{5,4},{6,7},{7,6},{8,9},{9,8},{10,11... | collective-permute-start | bytes 24584 | tf_op jit(solution)/shard_map/ppermute | solution.py:28
  14.9 0.1 stack_reshape.2
  15.0 2.5 %stack.3 = bf16[128,8,2048]{2,1,0:T(8,128)(2,1)} broadcast(bf16[8,2048]{1,0:T(8,128)(2,1)S(1)} %stack_reshape.2), dimensions={1,2} | broadcast | bytes 4227072 | tf_op jit(solution)/shard_map/stack | solution.py:105
  17.6 14.7 %all-to-all-start = ((bf16[128,8,2048]{2,1,0:T(8,128)(2,1)}), bf16[128,8,2048]{2,1,0:T(8,128)(2,1)}, u32[]{:S(2)}, u32[]{:S(2)}) async-start(bf16[128,8,2048]{2,1,0:T(8,128)(2,1)} %stack.3), calls=%async_computation | async-start | bytes 8388608 | tf_op jit(solution)/shard_map/all_to_all | solution.py:105
  32.4 2.4 %collective-permute-start = (bf16[36,1024]{1,0:T(8,128)(2,1)S(1)}, bf16[36,1024]{1,0:T(8,128)(2,1)S(1)}, u32[]{:S(2)}, u32[]{:S(2)}) collective-permute-start(bf16[36,1024]{1,0:T(8,128)(2,1)S(1)} %get-tuple-element.74), channel_id=1, source_target_pairs={{0,1},{1,2},{2,3},{3,4},{4,5},{5,6},{6,7},{7,8},{8,9},{9,10},{10,1... | collective-permute-start | bytes 221192 | tf_op jit(solution)/shard_map/ppermute | solution.py:19
  34.8 8.5 %collective-permute-start.1 = (bf16[36,1024]{1,0:T(8,128)(2,1)S(1)}, bf16[36,1024]{1,0:T(8,128)(2,1)S(1)}, u32[]{:S(2)}, u32[]{:S(2)}) collective-permute-start(bf16[36,1024]{1,0:T(8,128)(2,1)S(1)} %get-tuple-element.73), channel_id=1, source_target_pairs={{1,0},{2,1},{3,2},{4,3},{5,4},{6,5},{7,6},{8,7},{9,8},{10,9},{11,1... | collective-permute-start | bytes 221192 | tf_op jit(solution)/shard_map/ppermute | solution.py:20
  43.9 1.9 collective-permute-start.6
  46.0 1.9 collective-permute-start.7
  48.0 5.1 %collective-permute-done.7 = f32[32,64]{1,0:T(8,128)S(1)} collective-permute-done((f32[32,64]{1,0:T(8,128)S(1)}, f32[32,64]{1,0:T(8,128)S(1)}, u32[]{:S(2)}, u32[]{:S(2)}) %collective-permute-start.7) | collective-permute-done | bytes 8224 | tf_op jit(solution)/shard_map/ppermute | solution.py:28
  53.1 1.9 collective-permute-start.5
  55.2 65.8 %collective-permute-done.6 = f32[32,64]{1,0:T(8,128)S(1)} collective-permute-done((f32[32,64]{1,0:T(8,128)S(1)}, f32[32,64]{1,0:T(8,128)S(1)}, u32[]{:S(2)}, u32[]{:S(2)}) %collective-permute-start.6) | collective-permute-done | bytes 8224 | tf_op jit(solution)/shard_map/ppermute | solution.py:34
  120.9 6.6 %collective-permute-start.10 = (f32[32,64]{1,0:T(8,128)S(1)}, f32[32,64]{1,0:T(8,128)S(1)}, u32[]{:S(2)}, u32[]{:S(2)}) collective-permute-start(f32[32,64]{1,0:T(8,128)S(1)} %fusion.140), channel_id=1, source_target_pairs={{0,4},{1,5},{2,6},{3,7},{4,0},{5,1},{6,2},{7,3},{8,12},{9,13},{10,... | collective-permute-start | bytes 24584 | tf_op jit(solution)/shard_map/ppermute | solution.py:28
  127.7 0.7 collective-permute-done.10
  128.4 6.7 %collective-permute-start.9 = (f32[32,64]{1,0:T(8,128)S(1)}, f32[32,64]{1,0:T(8,128)S(1)}, u32[]{:S(2)}, u32[]{:S(2)}) collective-permute-start(f32[32,64]{1,0:T(8,128)S(1)} %select_add_fusion.1), channel_id=1, source_target_pairs={{8,0},{9,1},{10,2},{11,3},{12,4},{13,5},{14,6},{15,7},{16,8},{17,9... | collective-permute-start | bytes 24584 | tf_op jit(solution)/shard_map/ppermute | solution.py:34
  135.0 1.4 collective-permute-done.9
  136.4 8.9 %collective-permute-start.12 = (f32[32,64]{1,0:T(8,128)S(1)}, f32[32,64]{1,0:T(8,128)S(1)}, u32[]{:S(2)}, u32[]{:S(2)}) collective-permute-start(f32[32,64]{1,0:T(8,128)S(1)} %select_add_fusion), channel_id=1, source_target_pairs={{16,0},{17,1},{18,2},{19,3},{20,4},{21,5},{22,6},{23,7},{24,8},{25... | collective-permute-start | bytes 24584 | tf_op jit(solution)/shard_map/ppermute | solution.py:34
  145.5 1.3 collective-permute-done.12
  146.8 1.9 collective-permute-start.11
  148.8 8.1 %collective-permute-done.11 = f32[32,64]{1,0:T(8,128)S(1)} collective-permute-done((f32[32,64]{1,0:T(8,128)S(1)}, f32[32,64]{1,0:T(8,128)S(1)}, u32[]{:S(2)}, u32[]{:S(2)}) %collective-permute-start.11) | collective-permute-done | bytes 8224 | tf_op jit(solution)/shard_map/ppermute | solution.py:34
  156.9 1.9 collective-permute-start.8
  159.1 6.7 %collective-permute-done.8 = f32[32,64]{1,0:T(8,128)S(1)} collective-permute-done((f32[32,64]{1,0:T(8,128)S(1)}, f32[32,64]{1,0:T(8,128)S(1)}, u32[]{:S(2)}, u32[]{:S(2)}) %collective-permute-start.8) | collective-permute-done | bytes 8224 | tf_op jit(solution)/shard_map/ppermute | solution.py:34
  166.2 0.1 fusion.14
  166.5 0.1 fusion.16
  166.7 0.2 slice_reduce_fusion.27
  167.0 0.2 slice_reduce_fusion.19
  167.2 0.2 slice_reduce_fusion.11
  167.5 0.2 slice_reduce_fusion.3
  167.9 2.7 %convolution_multiply_fusion.7 = f32[8,256,32]{1,2,0:T(8,128)S(1)} fusion(f32[8,256]{1,0:T(8,128)S(1)} %sub.188, f32[8,256]{1,0:T(8,128)S(1)} %sub.186, f32[8,256]{1,0:T(8,128)S(1)} %sub.183, f32[8,256]{1,0:T(8,128)S(1)} %sub.181, f32[8,256]{1,0:T(8,128)S(1)} %sub.178, f32[8,256]{1,0:T(8,128)S(1)} %sub.176, f32[8,256]{1,0:T(8,128)S(1)} %mul.326, ...), kind=kOutput, calls=%fused_computation.28 | convolution fusion | flops 40960000 | bytes 458784 | tf_op jit(solution)/shard_map/rjl,jil->rji/dot_general | solution.py:87
  170.5 2.6 %fusion.8 = f32[8,256,32]{1,2,0:T(8,128)S(1)} fusion(f32[8,256,32]{1,2,0:T(8,128)S(1)} %convolution_multiply_fusion.7, f32[8,256]{1,0:T(8,128)S(1)} %sub.388, f32[8,256]{1,0:T(8,128)S(1)} %sub.385, f32[8,256]{1,0:T(8,128)S(1)} %sub.382, f32[8,256]{1,0:T(8,128)S(1)} %mul.337, f32[8,256]{1,0:T(8,128)S(1)} %sub.186, f32[8,256]{1,0:T(8,128)S(1)} %sub.181, ...), kind=kOutput, calls=%fused_computation.27 | convolution fusion | flops 41025536 | bytes 720928 | tf_op jit(solution)/shard_map/rjl,jil->rji/dot_general | solution.py:87
  173.2 2.6 %fusion.7 = f32[8,256,32]{1,2,0:T(8,128)S(1)} fusion(f32[8,256,32]{1,2,0:T(8,128)S(1)} %fusion.8, f32[8,256]{1,0:T(8,128)S(1)} %sub.397, f32[8,256]{1,0:T(8,128)S(1)} %sub.394, f32[8,256]{1,0:T(8,128)S(1)} %sub.391, f32[8,256]{1,0:T(8,128)S(1)} %mul.346, f32[8,256]{1,0:T(8,128)S(1)} %sub.186, f32[8,256]{1,0:T(8,128)S(1)} %sub.181, f32[8,256]{1,0:T(8,128)S(1)} %sub.176, ...), kind=kOutput, calls=%fused_computation.25 | convolution fusion | flops 41025536 | bytes 720928 | tf_op jit(solution)/shard_map/rjl,jil->rji/dot_general | solution.py:87
  175.8 2.6 %fusion.6 = f32[8,256,32]{1,2,0:T(8,128)S(1)} fusion(f32[8,256,32]{1,2,0:T(8,128)S(1)} %fusion.7, f32[8,256]{1,0:T(8,128)S(1)} %sub.406, f32[8,256]{1,0:T(8,128)S(1)} %sub.403, f32[8,256]{1,0:T(8,128)S(1)} %sub.400, f32[8,256]{1,0:T(8,128)S(1)} %mul.355, f32[8,256]{1,0:T(8,128)S(1)} %sub.186, f32[8,256]{1,0:T(8,128)S(1)} %sub.181, f32[8,256]{1,0:T(8,128)S(1)} %sub.176, ...), kind=kOutput, calls=%fused_computation.23 | convolution fusion | flops 41025536 | bytes 720928 | tf_op jit(solution)/shard_map/rjl,jil->rji/dot_general | solution.py:87
  178.4 2.6 %convolution_add_fusion = f32[8,256,32]{1,2,0:T(8,128)S(1)} fusion(f32[8,256,32]{1,2,0:T(8,128)S(1)} %fusion.6, f32[8,256]{1,0:T(8,128)S(1)} %sub.186, f32[8,256]{1,0:T(8,128)S(1)} %sub.181, f32[8,256]{1,0:T(8,128)S(1)} %sub.176, f32[8,256]{1,0:T(8,128)S(1)} %mul.324, bf16[4,8,8,256]{3,2,1,0:T(8,128)(2,1)S(1)} %bitcast.129), kind=kOutput, calls=%fused_computation.21 | convolution fusion | flops 40435712 | bytes 688128 | tf_op jit(solution)/shard_map/rjl,jil->rji/dot_general | solution.py:87
  181.1 2.6 %fusion.5 = f32[8,256,32]{1,2,0:T(8,128)S(1)} fusion(f32[8,256,32]{1,2,0:T(8,128)S(1)} %convolution_add_fusion, f32[8,256]{1,0:T(8,128)S(1)} %sub.421, f32[8,256]{1,0:T(8,128)S(1)} %sub.418, f32[8,256]{1,0:T(8,128)S(1)} %sub.415, f32[8,256]{1,0:T(8,128)S(1)} %mul.370, f32[8,256]{1,0:T(8,128)S(1)} %sub.186, f32[8,256]{1,0:T(8,128)S(1)} %sub.181, ...), kind=kOutput, calls=%fused_computation.20 | convolution fusion | flops 41025536 | bytes 720928 | tf_op jit(solution)/shard_map/rjl,jil->rji/dot_general | solution.py:87
  183.7 2.6 %fusion.4 = f32[8,256,32]{1,2,0:T(8,128)S(1)} fusion(f32[8,256,32]{1,2,0:T(8,128)S(1)} %fusion.5, f32[8,256]{1,0:T(8,128)S(1)} %sub.430, f32[8,256]{1,0:T(8,128)S(1)} %sub.427, f32[8,256]{1,0:T(8,128)S(1)} %sub.424, f32[8,256]{1,0:T(8,128)S(1)} %mul.380, f32[8,256]{1,0:T(8,128)S(1)} %sub.186, f32[8,256]{1,0:T(8,128)S(1)} %sub.181, f32[8,256]{1,0:T(8,128)S(1)} %sub.176, ...), kind=kOutput, calls=%fused_computation.18 | convolution fusion | flops 41025536 | bytes 720928 | tf_op jit(solution)/shard_map/rjl,jil->rji/dot_general | solution.py:87
  186.4 2.6 %fusion.3 = f32[8,256,32]{1,2,0:T(8,128)S(1)} fusion(f32[8,256,32]{1,2,0:T(8,128)S(1)} %fusion.4, f32[8,256]{1,0:T(8,128)S(1)} %sub.439, f32[8,256]{1,0:T(8,128)S(1)} %sub.436, f32[8,256]{1,0:T(8,128)S(1)} %sub.433, f32[8,256]{1,0:T(8,128)S(1)} %mul.390, f32[8,256]{1,0:T(8,128)S(1)} %sub.186, f32[8,256]{1,0:T(8,128)S(1)} %sub.181, f32[8,256]{1,0:T(8,128)S(1)} %sub.176, ...), kind=kOutput, calls=%fused_computation.16 | convolution fusion | flops 41025536 | bytes 720928 | tf_op jit(solution)/shard_map/rjl,jil->rji/dot_general | solution.py:87
  189.0 2.7 %fusion.2 = f32[32,8,256]{2,0,1:T(8,128)} fusion(f32[8,256,32]{1,2,0:T(8,128)S(1)} %fusion.3, f32[8,256]{1,0:T(8,128)S(1)} %sub.448, f32[8,256]{1,0:T(8,128)S(1)} %sub.445, f32[8,256]{1,0:T(8,128)S(1)} %sub.442, f32[8,256]{1,0:T(8,128)S(1)} %mul.400, f32[8,256]{1,0:T(8,128)S(1)} %sub.186, f32[8,256]{1,0:T(8,128)S(1)} %sub.181, f32[8,256]{1,0:T(8,128)S(1)} %sub.176, ...), kind=kOutput, calls=%fused_computation.14 | convolution fusion | flops 41025536 | bytes 720928 | tf_op jit(solution)/shard_map/rjl,jil->rji/dot_general | solution.py:87
  191.7 5.1 %gather_fusion = bf16[256,2048]{1,0:T(8,128)(2,1)S(1)} fusion(bf16[1024,2048]{1,0:T(8,128)(2,1)} %bitcast.1, s32[1024]{0:T(1024)S(1)} %pad_clamp_fusion), kind=kCustom, calls=%fused_computation | custom fusion | bytes 2098176 | tf_op jit(solution)/shard_map/gather | solution.py:107
  196.8 2.2 %reshape.389 = bf16[8,32,32,64]{3,2,1,0:T(8,128)(2,1)S(1)} reshape(bf16[256,2048]{1,0:T(8,128)(2,1)S(1)} %gather_fusion) | data formatting | bytes 2097152 | tf_op jit(solution)/shard_map/reshape | solution.py:108
  199.0 3.0 %convolution_bitcast_fusion.1 = f32[8,32,64]{2,1,0:T(8,128)S(1)} fusion(bf16[8,32,32,64]{3,2,1,0:T(8,128)(2,1)S(1)} %reshape.389, bf16[8,32,64,64]{3,2,1,0:T(8,128)(2,1)} %param.15), kind=kOutput, calls=%fused_computation.31 | convolution fusion | flops 67108864 | bytes 3211264 | tf_op jit(solution)/shard_map/jcrk,jckm->jrm/dot_general | solution.py:109
  202.1 0.5 fusion.12
  202.5 0.2 fusion.10
  202.7 0.7 copy.33
  (95 shorter events, 2.2 us)
Async XLA Ops:
  0.0 1.0 copy-start
  3.2 42.8 %collective-permute-start.3 = (f32[32,64]{1,0:T(8,128)S(1)}, f32[32,64]{1,0:T(8,128)S(1)}, u32[]{:S(2)}, u32[]{:S(2)}) collective-permute-start(f32[32,64]{1,0:T(8,128)S(1)} %convolution_bitcast_fusion.3), channel_id=1, source_target_pairs={{2,0},{3,1},{4,2},{5,3},{6,4},{7,5},{8,6},{9,7},{10,8},{11,9},{12,... | collective-permute-start | bytes 24584 | tf_op jit(solution)/shard_map/ppermute | solution.py:34
  9.5 156.9 %collective-permute-start.2 = (f32[32,64]{1,0:T(8,128)S(1)}, f32[32,64]{1,0:T(8,128)S(1)}, u32[]{:S(2)}, u32[]{:S(2)}) collective-permute-start(f32[32,64]{1,0:T(8,128)S(1)} %convolution_bitcast_fusion.3), channel_id=1, source_target_pairs={{0,2},{1,3},{2,4},{3,5},{4,6},{5,7},{6,8},{7,9},{8,10},{9,11},{10,... | collective-permute-start | bytes 24584 | tf_op jit(solution)/shard_map/ppermute | solution.py:34
  12.4 31.5 %collective-permute-start.4 = (f32[32,64]{1,0:T(8,128)S(1)}, f32[32,64]{1,0:T(8,128)S(1)}, u32[]{:S(2)}, u32[]{:S(2)}) collective-permute-start(f32[32,64]{1,0:T(8,128)S(1)} %fusion.154), channel_id=1, source_target_pairs={{0,1},{1,0},{2,3},{3,2},{4,5},{5,4},{6,7},{7,6},{8,9},{9,8},{10,11... | collective-permute-start | bytes 24584 | tf_op jit(solution)/shard_map/ppermute | solution.py:28
  17.5 14.8 %copy-start.1 = (bf16[32,2048]{1,0:T(8,128)(2,1)S(1)}, bf16[32,2048]{1,0:T(8,128)(2,1)}, u32[]{:S(2)}) copy-start(bf16[32,2048]{1,0:T(8,128)(2,1)} %param.9) | copy-start | bytes 393220
  17.5 14.8 %copy-start.5 = (bf16[4,2048]{1,0:T(4,128)(2,1)S(1)}, bf16[4,2048]{1,0:T(4,128)(2,1)}, u32[]{:S(2)}) copy-start(bf16[4,2048]{1,0:T(4,128)(2,1)} %param.10) | copy-start | bytes 49156
  17.5 25.9 %copy-start.6 = (s32[8,32]{1,0:T(8,128)S(1)}, s32[8,32]{1,0:T(8,128)}, u32[]{:S(2)}) copy-start(s32[8,32]{1,0:T(8,128)} %param.12) | copy-start | bytes 3076
  17.5 26.1 %copy-start.7 = (s32[8,4]{0,1:T(4,128)S(1)}, s32[8,4]{0,1:T(4,128)}, u32[]{:S(2)}) copy-start(s32[8,4]{0,1:T(4,128)} %param.11) | copy-start | bytes 388
  17.5 30.3 %copy-start.4 = (bf16[4,2,64,64]{3,2,1,0:T(8,128)(2,1)S(1)}, bf16[4,2,64,64]{3,2,1,0:T(8,128)(2,1)}, u32[]{:S(2)}) copy-start(bf16[4,2,64,64]{3,2,1,0:T(8,128)(2,1)} %param.17) | copy-start | bytes 196612
  17.6 174.1 %all-to-all-start = ((bf16[128,8,2048]{2,1,0:T(8,128)(2,1)}), bf16[128,8,2048]{2,1,0:T(8,128)(2,1)}, u32[]{:S(2)}, u32[]{:S(2)}) async-start(bf16[128,8,2048]{2,1,0:T(8,128)(2,1)} %stack.3), calls=%async_computation | async-start | bytes 8388608 | tf_op jit(solution)/shard_map/all_to_all | solution.py:105
  32.4 134.2 %collective-permute-start = (bf16[36,1024]{1,0:T(8,128)(2,1)S(1)}, bf16[36,1024]{1,0:T(8,128)(2,1)S(1)}, u32[]{:S(2)}, u32[]{:S(2)}) collective-permute-start(bf16[36,1024]{1,0:T(8,128)(2,1)S(1)} %get-tuple-element.74), channel_id=1, source_target_pairs={{0,1},{1,2},{2,3},{3,4},{4,5},{5,6},{6,7},{7,8},{8,9},{9,10},{10,1... | collective-permute-start | bytes 221192 | tf_op jit(solution)/shard_map/ppermute | solution.py:19
  34.8 131.8 %collective-permute-start.1 = (bf16[36,1024]{1,0:T(8,128)(2,1)S(1)}, bf16[36,1024]{1,0:T(8,128)(2,1)S(1)}, u32[]{:S(2)}, u32[]{:S(2)}) collective-permute-start(bf16[36,1024]{1,0:T(8,128)(2,1)S(1)} %get-tuple-element.73), channel_id=1, source_target_pairs={{1,0},{2,1},{3,2},{4,3},{5,4},{6,5},{7,6},{8,7},{9,8},{10,9},{11,1... | collective-permute-start | bytes 221192 | tf_op jit(solution)/shard_map/ppermute | solution.py:20
  43.9 77.1 %collective-permute-start.6 = (f32[32,64]{1,0:T(8,128)S(1)}, f32[32,64]{1,0:T(8,128)S(1)}, u32[]{:S(2)}, u32[]{:S(2)}) collective-permute-start(f32[32,64]{1,0:T(8,128)S(1)} %select_add_fusion.2), channel_id=1, source_target_pairs={{4,0},{5,1},{6,2},{7,3},{8,4},{9,5},{10,6},{11,7},{12,8},{13,9},{1... | collective-permute-start | bytes 24584 | tf_op jit(solution)/shard_map/ppermute | solution.py:34
  46.0 7.1 %collective-permute-start.7 = (f32[32,64]{1,0:T(8,128)S(1)}, f32[32,64]{1,0:T(8,128)S(1)}, u32[]{:S(2)}, u32[]{:S(2)}) collective-permute-start(f32[32,64]{1,0:T(8,128)S(1)} %fusion.147), channel_id=1, source_target_pairs={{0,2},{1,3},{2,0},{3,1},{4,6},{5,7},{6,4},{7,5},{8,10},{9,11},{10,... | collective-permute-start | bytes 24584 | tf_op jit(solution)/shard_map/ppermute | solution.py:28
  53.1 113.1 %collective-permute-start.5 = (f32[32,64]{1,0:T(8,128)S(1)}, f32[32,64]{1,0:T(8,128)S(1)}, u32[]{:S(2)}, u32[]{:S(2)}) collective-permute-start(f32[32,64]{1,0:T(8,128)S(1)} %select_add_fusion.2), channel_id=1, source_target_pairs={{0,4},{1,5},{2,6},{3,7},{4,8},{5,9},{6,10},{7,11},{8,12},{9,13},{1... | collective-permute-start | bytes 24584 | tf_op jit(solution)/shard_map/ppermute | solution.py:34
  120.9 7.4 %collective-permute-start.10 = (f32[32,64]{1,0:T(8,128)S(1)}, f32[32,64]{1,0:T(8,128)S(1)}, u32[]{:S(2)}, u32[]{:S(2)}) collective-permute-start(f32[32,64]{1,0:T(8,128)S(1)} %fusion.140), channel_id=1, source_target_pairs={{0,4},{1,5},{2,6},{3,7},{4,0},{5,1},{6,2},{7,3},{8,12},{9,13},{10,... | collective-permute-start | bytes 24584 | tf_op jit(solution)/shard_map/ppermute | solution.py:28
  128.4 8.1 %collective-permute-start.9 = (f32[32,64]{1,0:T(8,128)S(1)}, f32[32,64]{1,0:T(8,128)S(1)}, u32[]{:S(2)}, u32[]{:S(2)}) collective-permute-start(f32[32,64]{1,0:T(8,128)S(1)} %select_add_fusion.1), channel_id=1, source_target_pairs={{8,0},{9,1},{10,2},{11,3},{12,4},{13,5},{14,6},{15,7},{16,8},{17,9... | collective-permute-start | bytes 24584 | tf_op jit(solution)/shard_map/ppermute | solution.py:34
  136.4 10.4 %collective-permute-start.12 = (f32[32,64]{1,0:T(8,128)S(1)}, f32[32,64]{1,0:T(8,128)S(1)}, u32[]{:S(2)}, u32[]{:S(2)}) collective-permute-start(f32[32,64]{1,0:T(8,128)S(1)} %select_add_fusion), channel_id=1, source_target_pairs={{16,0},{17,1},{18,2},{19,3},{20,4},{21,5},{22,6},{23,7},{24,8},{25... | collective-permute-start | bytes 24584 | tf_op jit(solution)/shard_map/ppermute | solution.py:34
  146.8 10.1 %collective-permute-start.11 = (f32[32,64]{1,0:T(8,128)S(1)}, f32[32,64]{1,0:T(8,128)S(1)}, u32[]{:S(2)}, u32[]{:S(2)}) collective-permute-start(f32[32,64]{1,0:T(8,128)S(1)} %select_add_fusion), channel_id=1, source_target_pairs={{0,16},{1,17},{2,18},{3,19},{4,20},{5,21},{6,22},{7,23},{8,24},{9,... | collective-permute-start | bytes 24584 | tf_op jit(solution)/shard_map/ppermute | solution.py:34
  156.9 8.9 %collective-permute-start.8 = (f32[32,64]{1,0:T(8,128)S(1)}, f32[32,64]{1,0:T(8,128)S(1)}, u32[]{:S(2)}, u32[]{:S(2)}) collective-permute-start(f32[32,64]{1,0:T(8,128)S(1)} %select_add_fusion.1), channel_id=1, source_target_pairs={{0,8},{1,9},{2,10},{3,11},{4,12},{5,13},{6,14},{7,15},{8,16},{9,17... | collective-permute-start | bytes 24584 | tf_op jit(solution)/shard_map/ppermute | solution.py:34
  199.0 3.1 %copy-start.2 = (bf16[8,64,64]{2,1,0:T(8,128)(2,1)S(1)}, bf16[8,64,64]{2,1,0:T(8,128)(2,1)}, u32[]{:S(2)}) copy-start(bf16[8,64,64]{2,1,0:T(8,128)(2,1)} %param.14) | copy-start | bytes 196612
  199.0 3.5 %copy-start.3 = (f32[32,8,256]{2,0,1:T(8,128)S(1)}, f32[32,8,256]{2,0,1:T(8,128)}, u32[]{:S(2)}) copy-start(f32[32,8,256]{2,0,1:T(8,128)} %fusion.2) | copy-start | bytes 786436
